TPU v7x, 512 devices: a whole 4x8x8 slice. The times are simulated.
512 devices in a mesh: row: 16 (over y, core), col: 32 (over x, z).
Axes of the slice: x: 4, y: 8, z: 8, core: 2. Of those that a mesh axis runs over, the one named last changes fastest.
Arguments:
- tokens: bfloat16 [2304, 8192], P('col', 'row'), may hold values from -6 to 6
- out_grad: bfloat16 [2304, 8192], P('col', 'row'), may hold values from -6 to 6
- gate_pre: bfloat16 [2304, 12288], P('row', 'col'), may hold values from -8 to 8
- up_pre: bfloat16 [2304, 12288], P('row', 'col'), may hold values from -6 to 6
- w_gate: bfloat16 [8192, 12288], P('row', 'col'), may hold values from -0.0625 to 0.0625
- w_up: bfloat16 [8192, 12288], P('row', 'col'), may hold values from -0.0625 to 0.0625
- w_down: bfloat16 [12288, 8192], P('col', 'row'), may hold values from -0.0546875 to 0.0546875
Outputs:
- token_grad: bfloat16 [2304, 8192], P('col', 'row')
- gate_wgrad: bfloat16 [8192, 12288], P('row', 'col')
- up_wgrad: bfloat16 [8192, 12288], P('row', 'col')
- down_wgrad: bfloat16 [12288, 8192], P('col', 'row')
All inputs are finite; a program needn't handle non-finite values.
Results may differ from a plain program's by a relative error of at most 0.035.
Values may be sent and summed in bfloat16 or wider, within the bound.
No kernel may reach another device: no remote copies, remote signals or barrier semaphores. Data moves between devices by JAX's collectives and lax.ppermute only.
A program may use at most 64 MiB of HBM per device.

v0:
```python
import jax
import jax.numpy as jnp
from jax import lax
from jax.sharding import PartitionSpec as P


def contract_last(left_side, right_side):
    return lax.dot_general(
        left_side, right_side, (((1,), (1,)), ((), ())), preferred_element_type=jnp.float32
    )


def contract_first(left_side, right_side):
    return lax.dot_general(
        left_side, right_side, (((0,), (0,)), ((), ())), preferred_element_type=jnp.float32
    )


def swiglu_grads(hidden_grad, gate_pre, up_pre):
    gate_float = gate_pre.astype(jnp.float32)
    up_float = up_pre.astype(jnp.float32)
    sigmoid_gate = jax.nn.sigmoid(gate_float)
    swish_gate = gate_float * sigmoid_gate
    gate_grad = (
        hidden_grad * up_float * sigmoid_gate * (1.0 + gate_float * (1.0 - sigmoid_gate))
    ).astype(jnp.bfloat16)
    up_grad = (hidden_grad * swish_gate).astype(jnp.bfloat16)
    hidden = (swish_gate * up_float).astype(jnp.bfloat16)
    return (gate_grad, up_grad, hidden)


def local(tokens, out_grad, gate_pre, up_pre, w_gate, w_up, w_down):
    token_rows, grad_rows = (
        lax.all_gather(tokens, "col", axis=0, tiled=True),
        lax.all_gather(out_grad, "col", axis=0, tiled=True),
    )
    total_rows = grad_rows.shape[0]
    hidden_grad = lax.psum_scatter(
        contract_last(grad_rows, w_down).astype(jnp.bfloat16),
        "row",
        scatter_dimension=0,
        tiled=True,
    ).astype(jnp.float32)
    gate_share, up_share, hidden_share = swiglu_grads(hidden_grad, gate_pre, up_pre)
    gate_grad, up_grad, hidden = (
        lax.all_gather(gate_share, "row", axis=0, tiled=True),
        lax.all_gather(up_share, "row", axis=0, tiled=True),
        lax.all_gather(hidden_share, "row", axis=0, tiled=True),
    )
    token_grad = lax.psum_scatter(
        (contract_last(gate_grad, w_gate) + contract_last(up_grad, w_up)).astype(jnp.bfloat16),
        "col",
        scatter_dimension=0,
        tiled=True,
    )
    grad_scale = total_rows ** (-0.5)
    gate_wgrad = (contract_first(token_rows, gate_grad) * grad_scale).astype(jnp.bfloat16)
    up_wgrad = (contract_first(token_rows, up_grad) * grad_scale).astype(jnp.bfloat16)
    down_wgrad = (contract_first(hidden, grad_rows) * grad_scale).astype(jnp.bfloat16)
    return (token_grad, gate_wgrad, up_wgrad, down_wgrad)


def solution(mesh):
    return jax.shard_map(
        local,
        mesh=mesh,
        in_specs=(
            P("col", "row"),
            P("col", "row"),
            P("row", "col"),
            P("row", "col"),
            P("row", "col"),
            P("row", "col"),
            P("col", "row"),
        ),
        out_specs=(P("col", "row"), P("row", "col"), P("row", "col"), P("col", "row")),
        check_vma=False,
    )
```

profile of v0, /device:TPU:16, one launch (start us, length us, event | category | flops | bytes accessed | tf_op | source)
XLA Modules:
  0.0 613.3 jit_solution(11523516848758164644)
XLA Ops:
  7.2 0.0 copy-start
  7.2 0.0 all-gather.6.cloned.1.call-start
  7.2 0.7 all-gather.6.cloned.1.call-update
  7.9 0.0 copy-start.3
  7.9 0.0 copy-start.4
  7.9 0.0 reduce-scatter.3.cloned.1.call-start
  8.0 92.0 %all-gather.6.cloned.1.call-done = bf16[2304,512]{1,0:T(8,128)(2,1)} async-done(((bf16[72,512]{1,0:T(8,128)(2,1)}), bf16[2304,512]{1,0:T(8,128)(2,1)}) %all-gather.6.cloned.1.call-update) | async-done | bytes 2359312 | tf_op jit(solution)/shard_map/all_gather | solution.py:35
  99.9 4.4 convolution_convert_fusion
  104.3 0.0 reduce-scatter.3.cloned.1.call-update
  104.3 0.0 all-gather.8.cloned.1.call-start
  104.4 53.0 %reduce-scatter.3.cloned.1.call-done = bf16[144,384]{1,0:T(8,128)(2,1)} async-done(((bf16[2304,384]{1,0:T(8,128)(2,1)}), bf16[144,384]{1,0:T(8,128)(2,1)}) %reduce-scatter.3.cloned.1.call-update) | async-done | bytes 110608 | tf_op jit(solution)/shard_map/reduce_scatter | solution.py:38
  157.4 0.0 copy-done.3
  157.4 0.0 copy-done.4
  157.4 1.7 fusion.10
  159.1 0.0 all-gather.8.cloned.1.call-update
  159.2 0.0 all-gather.10.cloned.1.call-start
  159.2 0.5 all-gather.10.cloned.1.call-update
  159.7 0.0 all-gather.12.cloned.1.call-start
  159.8 0.5 all-gather.12.cloned.1.call-update
  160.3 0.0 all-gather.14.cloned.1.call-start
  160.4 0.5 all-gather.14.cloned.1.call-update
  160.9 0.0 copy-start.2
  160.9 0.0 reduce-scatter.5.cloned.1.call-start
  161.0 43.9 %all-gather.8.cloned.1.call-done = bf16[2304,384]{1,0:T(8,128)(2,1)} async-done(((bf16[144,384]{1,0:T(8,128)(2,1)}), bf16[2304,384]{1,0:T(8,128)(2,1)}) %all-gather.8.cloned.1.call-update) | async-done | bytes 1769488 | tf_op jit(solution)/shard_map/all_gather | solution.py:46
  204.9 0.0 copy-done
  204.9 5.0 fusion.15
  209.9 38.3 %all-gather.10.cloned.1.call-done = bf16[2304,384]{1,0:T(8,128)(2,1)} async-done(((bf16[144,384]{1,0:T(8,128)(2,1)}), bf16[2304,384]{1,0:T(8,128)(2,1)}) %all-gather.10.cloned.1.call-update) | async-done | bytes 1769488 | tf_op jit(solution)/shard_map/all_gather | solution.py:47
  248.2 0.0 copy-done.2
  248.2 5.7 fusion
  253.9 0.0 copy-start.1
  253.9 0.0 reduce-scatter.5.cloned.1.call-update
  253.9 82.2 %all-gather.12.cloned.1.call-done = bf16[2304,512]{1,0:T(8,128)(2,1)} async-done(((bf16[72,512]{1,0:T(8,128)(2,1)}), bf16[2304,512]{1,0:T(8,128)(2,1)}) %all-gather.12.cloned.1.call-update) | async-done | bytes 2359312 | tf_op jit(solution)/shard_map/all_gather | solution.py:34
  336.1 0.0 copy-done.1
  336.1 2.8 fusion.5
  338.9 0.9 copy.11
  339.8 0.0 copy-start.5
  339.8 3.5 fusion.4
  343.3 0.9 copy.12
  344.2 32.2 %all-gather.14.cloned.1.call-done = bf16[2304,384]{1,0:T(8,128)(2,1)} async-done(((bf16[144,384]{1,0:T(8,128)(2,1)}), bf16[2304,384]{1,0:T(8,128)(2,1)}) %all-gather.14.cloned.1.call-update) | async-done | bytes 1769488 | tf_op jit(solution)/shard_map/all_gather | solution.py:48
  376.3 0.0 copy-done.5
  376.3 3.3 fusion.3
  379.7 226.8 %reduce-scatter.5.cloned.1.call-done = bf16[72,512]{1,0:T(8,128)(2,1)} async-done(((bf16[2304,512]{1,0:T(8,128)(2,1)}), bf16[72,512]{1,0:T(8,128)(2,1)}) %reduce-scatter.5.cloned.1.call-update) | async-done | bytes 73744 | tf_op jit(solution)/shard_map/reduce_scatter | solution.py:50
Async XLA Ops:
  7.2 197.7 %copy-start = (bf16[512,384]{1,0:T(8,128)(2,1)S(1)}, bf16[512,384]{1,0:T(8,128)(2,1)}, u32[]{:S(2)}) copy-start(bf16[512,384]{1,0:T(8,128)(2,1)} %param.11) | copy-start | bytes 1179652
  7.2 92.8 %all-gather.6.cloned.1.call-start = ((), (), s32[]{:S(2)}) async-start(), calls=%async_computation.2 | async-start | bytes 2433024 | tf_op jit(solution)/shard_map/all_gather | solution.py:35
  7.9 149.5 %copy-start.3 = (bf16[144,384]{1,0:T(8,128)(2,1)S(1)}, bf16[144,384]{1,0:T(8,128)(2,1)}, u32[]{:S(2)}) copy-start(bf16[144,384]{1,0:T(8,128)(2,1)} %param.10) | copy-start | bytes 331780
  7.9 149.5 %copy-start.4 = (bf16[144,384]{1,0:T(8,128)(2,1)S(1)}, bf16[144,384]{1,0:T(8,128)(2,1)}, u32[]{:S(2)}) copy-start(bf16[144,384]{1,0:T(8,128)(2,1)} %param.9) | copy-start | bytes 331780
  7.9 149.4 %reduce-scatter.3.cloned.1.call-start = ((), (), s32[]{:S(2)}) async-start(), calls=%async_computation.3 | async-start | bytes 1880064 | tf_op jit(solution)/shard_map/reduce_scatter | solution.py:38
  104.3 100.5 %all-gather.8.cloned.1.call-start = ((), (), s32[]{:S(2)}) async-start(), calls=%async_computation.4 | async-start | bytes 1880064 | tf_op jit(solution)/shard_map/all_gather | solution.py:46
  159.2 89.1 %all-gather.10.cloned.1.call-start = ((), (), s32[]{:S(2)}) async-start(), calls=%async_computation.5 | async-start | bytes 1880064 | tf_op jit(solution)/shard_map/all_gather | solution.py:47
  159.7 176.4 %all-gather.12.cloned.1.call-start = ((), (), s32[]{:S(2)}) async-start(), calls=%async_computation.7 | async-start | bytes 2433024 | tf_op jit(solution)/shard_map/all_gather | solution.py:34
  160.3 216.0 %all-gather.14.cloned.1.call-start = ((), (), s32[]{:S(2)}) async-start(), calls=%async_computation.8 | async-start | bytes 1880064 | tf_op jit(solution)/shard_map/all_gather | solution.py:48
  160.9 87.3 %copy-start.2 = (bf16[512,384]{1,0:T(8,128)(2,1)S(1)}, bf16[512,384]{1,0:T(8,128)(2,1)}, u32[]{:S(2)}) copy-start(bf16[512,384]{1,0:T(8,128)(2,1)} %param.12) | copy-start | bytes 1179652
  160.9 445.5 %reduce-scatter.5.cloned.1.call-start = ((), (), s32[]{:S(2)}) async-start(), calls=%async_computation.6 | async-start | bytes 2433024 | tf_op jit(solution)/shard_map/reduce_scatter | solution.py:50
  253.9 82.2 %copy-start.1 = (bf16[2304,384]{1,0:T(8,128)(2,1)S(1)}, bf16[2304,384]{1,0:T(8,128)(2,1)}, u32[]{:S(2)}) copy-start(bf16[2304,384]{1,0:T(8,128)(2,1)} %all-gather.8.cloned.1.call-done) | copy-start | bytes 5308420
  339.8 36.6 %copy-start.5 = (bf16[2304,512]{1,0:T(8,128)(2,1)S(1)}, bf16[2304,512]{1,0:T(8,128)(2,1)}, u32[]{:S(2)}) copy-start(bf16[2304,512]{1,0:T(8,128)(2,1)} %all-gather.6.cloned.1.call-done) | copy-start | bytes 7077892
Sparse Core Ops, SparseCore 0:
  11.2 88.7 all-gather.5
  104.5 52.8 reduce-scatter.2
  160.3 44.5 all-gather.7
  207.6 40.5 all-gather.9
  251.7 84.3 all-gather.11
  338.9 37.4 all-gather.13
  382.0 224.4 reduce-scatter.4
where the time goes:
time: 614 us; the launch traced here: 613 us
  waiting for transfers between devices  571 us (93%)
  matrix products  24.6 us (4%)
  between operations  14.2 us (2%)
    reduce_scatter x1, waiting for transfers between devices, local(): lax.psum_scatter((contract_last(gate_grad, w_gate) + contract_last(up_gra...  227 us
    all_gather x1, waiting for transfers between devices, local(): lax.all_gather(out_grad, 'col', axis=0, tiled=True)  92 us
    all_gather x1, waiting for transfers between devices, local(): lax.all_gather(tokens, 'col', axis=0, tiled=True)  82.2 us
    reduce_scatter x1, waiting for transfers between devices, local(): lax.psum_scatter(contract_last(grad_rows, w_down).astype(jnp.bfloat16), '...  53 us
    all_gather x1, waiting for transfers between devices, local(): lax.all_gather(gate_share, 'row', axis=0, tiled=True)  43.9 us
    all_gather x1, waiting for transfers between devices, local(): lax.all_gather(up_share, 'row', axis=0, tiled=True)  38.3 us
    all_gather x1, waiting for transfers between devices, local(): lax.all_gather(hidden_share, 'row', axis=0, tiled=True)  32.2 us
    dot_general x3, matrix products, contract_last(): lax.dot_general(left_side, right_side, (((1,), (1,)), ((), ())), preferre...  15.1 us
  transfers between devices with their start and end apart: 7, of which 7 were waited for; matrix products, arithmetic and copies ran while one was open for 4% of the time, Pallas kernels for 0%

commit v1 on v0

--- a/solution.py
+++ b/solution.py
@@ -2,6 +2,13 @@
 import jax.numpy as jnp
 from jax import lax
 from jax.sharding import PartitionSpec as P
+
+
+def gather_over(block, axis, along):
+    n_dev = lax.axis_size(axis)
+    tiles = jnp.stack([block for _ in range(n_dev)])
+    tiles = lax.all_to_all(tiles, axis, split_axis=0, concat_axis=0)
+    return jnp.concatenate(tiles, axis=along)
 
 
 def contract_last(left_side, right_side):
@@ -43,7 +50,7 @@
     ).astype(jnp.float32)
     gate_share, up_share, hidden_share = swiglu_grads(hidden_grad, gate_pre, up_pre)
     gate_grad, up_grad, hidden = (
-        lax.all_gather(gate_share, "row", axis=0, tiled=True),
+        gather_over(gate_share, "row", 0),
         lax.all_gather(up_share, "row", axis=0, tiled=True),
         lax.all_gather(hidden_share, "row", axis=0, tiled=True),
     )

time: 614 us -> 590 us (0.961)
  the two profiles are of different devices: /device:TPU:16 before, /device:TPU:8 now
where the time goes in v1:
time: 590 us
  waiting for transfers between devices  539 us (91%)
  matrix products  23.7 us (4%)
  between operations  14.2 us (2%)
  starting transfers between devices  8.31 us (1%)
    reduce_scatter x1, waiting for transfers between devices, local(): lax.psum_scatter((contract_last(gate_grad, w_gate) + contract_last(up_gra...  225 us
    all_gather x1, waiting for transfers between devices, local(): lax.all_gather(out_grad, 'col', axis=0, tiled=True)  92.1 us
    all_gather x1, waiting for transfers between devices, local(): lax.all_gather(tokens, 'col', axis=0, tiled=True)  84.3 us
    reduce_scatter x1, waiting for transfers between devices, local(): lax.psum_scatter(contract_last(grad_rows, w_down).astype(jnp.bfloat16), '...  55 us
    all_to_all x1, waiting for transfers between devices, gather_over(): tiles = lax.all_to_all(tiles, axis, split_axis=0, concat_axis=0)  46.7 us
    all_gather x1, waiting for transfers between devices, local(): lax.all_gather(hidden_share, 'row', axis=0, tiled=True)  33.1 us
    dot_general x3, matrix products, contract_last(): lax.dot_general(left_side, right_side, (((1,), (1,)), ((), ())), preferre...  13.6 us
  transfers between devices with their start and end apart: 7, of which 7 were waited for; matrix products, arithmetic and copies ran while one was open for 4% of the time, Pallas kernels for 0%

profile of v1, /device:TPU:8, one launch (start us, length us, event | category | flops | bytes accessed | tf_op | source)
XLA Modules:
  0.0 590.2 jit_solution(165388246930538357)
XLA Ops:
  7.2 0.0 copy-start
  7.2 0.0 all-gather.5.cloned.1.call-start
  7.2 0.7 all-gather.5.cloned.1.call-update
  7.9 0.0 copy-start.2
  7.9 0.0 copy-start.3
  7.9 0.0 reduce-scatter.3.cloned.1.call-start
  8.0 92.1 %all-gather.5.cloned.1.call-done = bf16[2304,512]{1,0:T(8,128)(2,1)} async-done(((bf16[72,512]{1,0:T(8,128)(2,1)}), bf16[2304,512]{1,0:T(8,128)(2,1)}) %all-gather.5.cloned.1.call-update) | async-done | bytes 2359312 | tf_op jit(solution)/shard_map/all_gather | solution.py:42
  100.0 4.4 convolution_convert_fusion
  104.4 0.0 reduce-scatter.3.cloned.1.call-update
  104.4 0.0 all-gather.7.cloned.1.call-start
  104.5 55.0 %reduce-scatter.3.cloned.1.call-done = bf16[144,384]{1,0:T(8,128)(2,1)} async-done(((bf16[2304,384]{1,0:T(8,128)(2,1)}), bf16[144,384]{1,0:T(8,128)(2,1)}) %reduce-scatter.3.cloned.1.call-update) | async-done | bytes 110608 | tf_op jit(solution)/shard_map/reduce_scatter | solution.py:45
  159.4 0.0 copy-done.2
  159.4 0.0 copy-done.3
  159.5 1.7 fusion.10
  161.2 0.0 all-gather.7.cloned.1.call-update
  161.2 0.0 all-gather.9.cloned.1.call-start
  161.2 0.5 all-gather.9.cloned.1.call-update
  161.8 1.4 stack.2
  163.1 8.1 %all-to-all-start = ((bf16[16,144,384]{2,1,0:T(8,128)(2,1)}), bf16[16,144,384]{2,1,0:T(8,128)(2,1)S(1)}, u32[]{:S(2)}, u32[]{:S(2)}) async-start(bf16[16,144,384]{2,1,0:T(8,128)(2,1)} %stack.2), calls=%async_computation.1 | async-start | bytes 3538944 | tf_op jit(solution)/shard_map/all_to_all | solution.py:10
  171.2 0.0 all-gather.11.cloned.1.call-start
  171.3 0.5 all-gather.11.cloned.1.call-update
  171.8 0.0 reduce-scatter.5.cloned.1.call-start
  171.9 46.7 %all-to-all-done = bf16[16,144,384]{2,1,0:T(8,128)(2,1)S(1)} async-done(((bf16[16,144,384]{2,1,0:T(8,128)(2,1)}), bf16[16,144,384]{2,1,0:T(8,128)(2,1)S(1)}, u32[]{:S(2)}, u32[]{:S(2)}) %all-to-all-start) | async-done | bytes 1769504 | tf_op jit(solution)/shard_map/all_to_all | solution.py:10
  218.5 0.0 copy-done
  218.5 0.0 copy-start.1
  218.5 3.5 fusion.15
  222.1 1.1 all-gather.7.cloned.1.call-done
  223.2 0.0 copy-done.1
  223.2 5.7 fusion
  228.9 0.0 reduce-scatter.5.cloned.1.call-update
  228.9 84.3 %all-gather.9.cloned.1.call-done = bf16[2304,512]{1,0:T(8,128)(2,1)} async-done(((bf16[72,512]{1,0:T(8,128)(2,1)}), bf16[2304,512]{1,0:T(8,128)(2,1)}) %all-gather.9.cloned.1.call-update) | async-done | bytes 2359312 | tf_op jit(solution)/shard_map/all_gather | solution.py:41
  313.2 3.3 fusion.4
  316.5 0.9 copy.12
  317.4 2.8 fusion.5
  320.2 0.9 copy.11
  321.1 33.1 %all-gather.11.cloned.1.call-done = bf16[2304,384]{1,0:T(8,128)(2,1)} async-done(((bf16[144,384]{1,0:T(8,128)(2,1)}), bf16[2304,384]{1,0:T(8,128)(2,1)}) %all-gather.11.cloned.1.call-update) | async-done | bytes 1769488 | tf_op jit(solution)/shard_map/all_gather | solution.py:55
  354.2 4.1 fusion.3
  358.3 225.1 %reduce-scatter.5.cloned.1.call-done = bf16[72,512]{1,0:T(8,128)(2,1)} async-done(((bf16[2304,512]{1,0:T(8,128)(2,1)}), bf16[72,512]{1,0:T(8,128)(2,1)}) %reduce-scatter.5.cloned.1.call-update) | async-done | bytes 73744 | tf_op jit(solution)/shard_map/reduce_scatter | solution.py:57
Async XLA Ops:
  7.2 211.4 %copy-start = (bf16[512,384]{1,0:T(8,128)(2,1)S(1)}, bf16[512,384]{1,0:T(8,128)(2,1)}, u32[]{:S(2)}) copy-start(bf16[512,384]{1,0:T(8,128)(2,1)} %param.11) | copy-start | bytes 1179652
  7.2 92.9 %all-gather.5.cloned.1.call-start = ((), (), s32[]{:S(2)}) async-start(), calls=%async_computation.3 | async-start | bytes 2433024 | tf_op jit(solution)/shard_map/all_gather | solution.py:42
  7.9 151.5 %copy-start.2 = (bf16[144,384]{1,0:T(8,128)(2,1)S(1)}, bf16[144,384]{1,0:T(8,128)(2,1)}, u32[]{:S(2)}) copy-start(bf16[144,384]{1,0:T(8,128)(2,1)} %param.10) | copy-start | bytes 331780
  7.9 151.5 %copy-start.3 = (bf16[144,384]{1,0:T(8,128)(2,1)S(1)}, bf16[144,384]{1,0:T(8,128)(2,1)}, u32[]{:S(2)}) copy-start(bf16[144,384]{1,0:T(8,128)(2,1)} %param.9) | copy-start | bytes 331780
  7.9 151.5 %reduce-scatter.3.cloned.1.call-start = ((), (), s32[]{:S(2)}) async-start(), calls=%async_computation.4 | async-start | bytes 1880064 | tf_op jit(solution)/shard_map/reduce_scatter | solution.py:45
  104.4 118.8 %all-gather.7.cloned.1.call-start = ((), (), s32[]{:S(2)}) async-start(), calls=%async_computation.5 | async-start | bytes 1880064 | tf_op jit(solution)/shard_map/all_gather | solution.py:54
  161.2 152.0 %all-gather.9.cloned.1.call-start = ((), (), s32[]{:S(2)}) async-start(), calls=%async_computation.7 | async-start | bytes 2433024 | tf_op jit(solution)/shard_map/all_gather | solution.py:41
  163.1 55.4 %all-to-all-start = ((bf16[16,144,384]{2,1,0:T(8,128)(2,1)}), bf16[16,144,384]{2,1,0:T(8,128)(2,1)S(1)}, u32[]{:S(2)}, u32[]{:S(2)}) async-start(bf16[16,144,384]{2,1,0:T(8,128)(2,1)} %stack.2), calls=%async_computation.1 | async-start | bytes 3538944 | tf_op jit(solution)/shard_map/all_to_all | solution.py:10
  171.2 183.0 %all-gather.11.cloned.1.call-start = ((), (), s32[]{:S(2)}) async-start(), calls=%async_computation.8 | async-start | bytes 1880064 | tf_op jit(solution)/shard_map/all_gather | solution.py:55
  171.8 411.5 %reduce-scatter.5.cloned.1.call-start = ((), (), s32[]{:S(2)}) async-start(), calls=%async_computation.6 | async-start | bytes 2433024 | tf_op jit(solution)/shard_map/reduce_scatter | solution.py:57
  218.5 4.7 copy-start.1
Sparse Core Ops, SparseCore 0:
  11.2 88.8 all-gather.4
  104.6 54.8 reduce-scatter.2
  162.4 60.7 all-gather.6
  226.7 86.4 all-gather.8
  316.0 38.1 all-gather.10
  359.7 223.5 reduce-scatter.4
